TPU v7x, 32 devices: a whole 2x2x4 slice. The times are simulated.
32 devices in a mesh: section: 8 (over y, x, core), shard: 4 (over z).
Axes of the slice: x: 2, y: 2, z: 4, core: 2. Of those that a mesh axis runs over, the one named last changes fastest.
Arguments:
- tokens: bfloat16 [64, 1024, 512], P(('section', 'shard')), may hold values from -6 to 6
- cotangent: bfloat16 [64, 1024, 512], P(('section', 'shard')), may hold values from -6 to 6
- route: int32 [32, 1024], replicated, may hold values from 0 to 1, as said below
- remask: int32 [32, 1024], replicated, may hold values 0 or 1
- timestep: int32 [32], replicated, may hold values from 0 to 49
- enc_qkv: float32 [512, 1536], P('shard'), may hold values from -0.25 to 0.25
- enc_out: float32 [512, 512], P('shard'), may hold values from -2 to 2
- enc_up: float32 [512, 2048], P('shard'), may hold values from -0.25 to 0.25
- enc_down: float32 [2048, 512], P('shard'), may hold values from -0.125 to 0.125
- enc_gains: float32 [2, 512], P(None, 'shard'), may hold values from 0.5 to 1.5
- enc_shifts: float32 [2, 512], P(None, 'shard'), may hold values from -4 to 4
- dec_qkv: float32 [512, 1536], P('shard'), may hold values from -0.25 to 0.25
- dec_out: float32 [512, 512], P('shard'), may hold values from -2 to 2
- cross_query: float32 [512, 512], P('shard'), may hold values from -0.25 to 0.25
- cross_kv: float32 [512, 1024], P('shard'), may hold values from -0.25 to 0.25
- cross_out: float32 [512, 512], P('shard'), may hold values from -2 to 2
- dec_up: float32 [512, 2048], P('shard'), may hold values from -0.25 to 0.25
- dec_down: float32 [2048, 512], P('shard'), may hold values from -0.125 to 0.125
- dec_gains: float32 [3, 512], P(None, 'shard'), may hold values from 0.5 to 1.5
- dec_shifts: float32 [3, 512], P(None, 'shard'), may hold values from -4 to 4
- time_table: float32 [50, 512], P(None, 'shard'), may hold values from -6 to 6
- mask_embed: float32 [512], P('shard'), may hold values from -6 to 6
Outputs:
- layer_out: bfloat16 [64, 1024, 512], P(('section', 'shard'))
- grad_in: float32 [64, 1024, 512], P(('section', 'shard'))
- grad_enc_qkv: float32 [512, 1536], P('shard')
- grad_enc_out: float32 [512, 512], P('shard')
- grad_enc_up: float32 [512, 2048], P('shard')
- grad_enc_down: float32 [2048, 512], P('shard')
- grad_enc_gains: float32 [2, 512], P(None, 'shard')
- grad_enc_shifts: float32 [2, 512], P(None, 'shard')
- grad_dec_qkv: float32 [512, 1536], P('shard')
- grad_dec_out: float32 [512, 512], P('shard')
- grad_cross_query: float32 [512, 512], P('shard')
- grad_cross_kv: float32 [512, 1024], P('shard')
- grad_cross_out: float32 [512, 512], P('shard')
- grad_dec_up: float32 [512, 2048], P('shard')
- grad_dec_down: float32 [2048, 512], P('shard')
- grad_dec_gains: float32 [3, 512], P(None, 'shard')
- grad_dec_shifts: float32 [3, 512], P(None, 'shard')
- grad_time_table: float32 [50, 512], P(None, 'shard')
- grad_mask_embed: float32 [512], P('shard')
Inputs may be any that keep to these rules, and one draw needn't show every extreme that they name: route is 1 at the first token of every sequence.
All inputs are finite; a program needn't handle non-finite values.
Results may differ from a plain program's by a relative error of at most 0.024.
The roundings to bfloat16 on the way count: a program that leaves them out, or rounds other values in their place, can miss the bound.
Values may be sent and summed in bfloat16 or wider, within the bound.
A program may use at most 320 MiB of HBM per device.

v0:
```python
import functools

import jax
import jax.numpy as jnp
from jax import lax
from jax.experimental import pallas as pl
from jax.experimental.pallas import tpu as pltpu
from jax.sharding import PartitionSpec as P

HEADS = 8
EPSILON = 1e-05
BF = jnp.bfloat16
F32 = jnp.float32
NN = (((1,), (0,)), ((), ()))
NT = (((1,), (1,)), ((), ()))
TN = (((0,), (0,)), ((), ()))
RB = 256
AB = 512
LANES = 128
WIDTH = 512
MASK_ROW = 10
STEP_ROW = 11
VEC_ROWS = 12
MASK_LANE = 8
SCALE_LANE = 9
SMALL_ROWS = 64
OWNED = 7
UNITS = 12
ITEMS = 10
MESH = pl.DeviceIdType.MESH


def dot(left, right, dims=NN):
    return lax.dot_general(left, right, dims, preferred_element_type=F32)


def rows_at(r, count=RB):
    return pl.ds(pl.multiple_of(r * count, count), count)


def lanes_at(c, count=LANES):
    return pl.ds(pl.multiple_of(c * count, count), count)


def low_half(shape):
    return lax.broadcasted_iota(jnp.int32, shape, 1) < LANES // 2


def norm_rows(value):
    average = jnp.mean(value, axis=-1, keepdims=True)
    centred = value - average
    spread = jnp.mean(centred * centred, axis=-1, keepdims=True)
    inverse = lax.rsqrt(spread + EPSILON)
    return centred * inverse, inverse


def norm_rows_back(upstream, normal, inverse, gain):
    scaled = upstream * gain
    first = jnp.mean(scaled, axis=-1, keepdims=True)
    second = jnp.mean(scaled * normal, axis=-1, keepdims=True)
    return inverse * (scaled - first - normal * second)


def gelu_both(p):
    a = 0.7978845608028654
    b = 0.044715
    u = p * (a + (a * b) * (p * p))
    half = 0.5 + 0.5 * jnp.tanh(u)
    slope = half + (half - half * half) * (6.0 * u - (4.0 * a) * p)
    return p * half, slope


def kernel(
    x_in, cot_in, route, remask, timestep,
    enc_qkv, enc_out, enc_up, enc_down, dec_qkv, dec_out,
    cross_query, cross_kv, cross_out, dec_up, dec_down,
    enc_gains, enc_shifts, dec_gains, dec_shifts, mask_embed, time_table,
    lo, gin, gout, gv, p_hbm, f_hbm, cot_land, out_land, gin_land, h_land,
    wa, wu, wd, small, vec, pick, marks,
    gacc, x, qkv, oa, xh, rs, hb, res, dfb, dob, big, dp, kvt, gs,
    r0, r1, r2, r3s, r3r, sg, sgr, sgz,
    send_sem, recv_sem, load_sem, small_sem, swap_sem,
    cot_sem, h_sem, big_sem, lo_sem, gin_sem, rs_send, rs_recv, rs_keep, sg_send, sg_recv, free,
):
    length, features = x.shape[1], x.shape[2]
    hidden = wu.shape[2]
    blocks = length // RB
    pairs = features // LANES
    width = features
    section = lax.axis_index("section")
    role = (section >= lax.axis_size("section") // 2).astype(jnp.int32)
    own, other = role, 1 - role
    sections, shards = lax.axis_size("section"), lax.axis_size("shard")
    shard = lax.axis_index("shard")
    core = lax.rem(section, 2)
    side = lax.rem(section // 2, 2)
    quarter = 2 * core + side
    core_peer = (section + 1 - 2 * core, shard)
    side_peer = (section + 2 - 4 * side, shard)
    turns = range(1, shards)

    def bit_peer(bit):
        return (section + bit * (1 - 2 * lax.rem(section // bit, 2)), shard)

    far_peers = [bit_peer(4 << b) for b in range((sections // 4).bit_length() - 1)]
    half_peer = far_peers[-1]

    def later(k):
        return lax.rem(shard + k, shards)

    items = [(wa, own, slice(c * width, (c + 1) * width)) for c in range(4)] + [
        (wa, other, slice(0, 4 * width)),
        (wu, 0, slice(0, hidden)),
        (wd, 0, slice(0, width)),
        (wa, 2, slice(0, 4 * width)),
        (wu, 1, slice(0, hidden)),
        (wd, 1, slice(0, width)),
    ]

    block_rows = width // shards

    def columns(*refs):
        return [
            ref.at[:, c * width : (c + 1) * width] for ref in refs for c in range(ref.shape[1] // width)
        ]

    def row_blocks(ref):
        return [ref.at[j * block_rows : (j + 1) * block_rows, :] for j in range(shards)]

    masters = [
        columns(enc_qkv, enc_out), columns(dec_qkv, dec_out), columns(enc_up), row_blocks(enc_down),
        columns(cross_query, cross_kv, cross_out), columns(dec_up), row_blocks(dec_down),
    ]

    def staged(unit, j):
        if unit == 4:
            return kvt.at[j // 2, 0:block_rows, (j % 2) * width : (j % 2 + 1) * width]
        half, start = [(0, 0), (0, 1), (1, 0), (1, 1), None, (0, 0), (0, 1)][unit]
        first = start * 4 * block_rows + j * block_rows
        return res.at[half, first : first + block_rows, :]

    def load_master(unit, j):
        return pltpu.make_async_copy(masters[unit][j], staged(unit, j), load_sem.at[unit, j])

    def load_masters(unit):
        for j in range(4):
            load_master(unit, j).start()

    def round_master(unit, full, lead, by_rows=False):
        for j in range(4):
            load_master(unit, j).wait()
            value = staged(unit, j)[...].astype(BF)
            if by_rows:
                first = shard * (4 * block_rows) + j * block_rows
                full[lead, pl.ds(pl.multiple_of(first, block_rows), block_rows), :] = value
            else:
                first = pl.multiple_of(shard * block_rows, block_rows)
                full[lead, pl.ds(first, block_rows), j * width : (j + 1) * width] = value

    def round_layer(layer):
        for j in range(4):
            first = pl.multiple_of(layer * (4 * block_rows) + j * block_rows, block_rows)
            place = res.at[0, pl.ds(first, block_rows), :]
            pltpu.make_async_copy(place, place, load_sem.at[layer, j]).wait()
            rows = pl.ds(pl.multiple_of(shard * block_rows, block_rows), block_rows)
            wa[layer, rows, j * width : (j + 1) * width] = place[...].astype(BF)

    def remote(src, dst, sems, peer):
        return pltpu.make_async_remote_copy(
            src_ref=src, dst_ref=dst, send_sem=send_sem.at[sems], recv_sem=recv_sem.at[sems],
            device_id=peer, device_id_type=MESH,
        )

    def piece(item, owner, first, count):
        full, lead, cols = items[item]
        size = full.shape[1] // (4 * shards)
        start = pl.multiple_of(owner * (4 * size) + first * size, size)
        return full.at[lead, pl.ds(start, count * size), cols]

    def hop(item, stage, k):
        if stage == 0:
            src = piece(item, shard, quarter, 1)
            return src, src, (section, later(k))
        if stage == 1:
            src = piece(item, later(k), quarter, 1)
            return src, src, side_peer
        src = piece(item, later(k), 2 * core, 2)
        return src, src, core_peer

    def arrival(item, stage, k):
        if stage == 0:
            return piece(item, later(shards - k), quarter, 1)
        if stage == 1:
            return piece(item, later(k), 2 * core + 1 - side, 1)
        return piece(item, later(k), 2 - 2 * core, 2)

    def send(item, stage):
        for k in turns:
            src, dst, peer = hop(item, stage, k)
            remote(src, dst, (item, stage, k - 1), peer).start()

    def take(item, stage):
        for k in turns:
            dst = arrival(item, stage, k)
            remote(dst, dst, (item, stage, k - 1), core_peer).wait_recv()

    def small_copy(k):
        return pltpu.make_async_remote_copy(
            src_ref=small.at[shard], dst_ref=small.at[shard], send_sem=small_sem.at[0, k - 1],
            recv_sem=small_sem.at[1, k - 1], device_id=(section, later(k)), device_id_type=MESH,
        )

    QUARTERS = 4

    def part_rows(i):
        return slice(i * length // QUARTERS, (i + 1) * length // QUARTERS)

    def send_lo(source, i):
        return swap_copy(source.at[part_rows(i), :], lo.at[own, part_rows(i), :], 2 + i)

    def send_gin(i):
        return swap_copy(dp.at[part_rows(i), :], gin_land.at[part_rows(i), :], 2 + QUARTERS + i)

    def swap_copy(src, dst, index):
        return pltpu.make_async_remote_copy(
            src_ref=src, dst_ref=dst, send_sem=swap_sem.at[0, index], recv_sem=swap_sem.at[1, index],
            device_id=half_peer, device_id_type=MESH,
        )

    def for_rows(body):
        def step(r, carry):
            body(rows_at(r))
            return carry

        lax.fori_loop(0, blocks, step, 0)

    lane_ids = lax.broadcasted_iota(jnp.int32, (RB, LANES), 1)

    def keep_inverse(index, rows, inverse):
        rs[rows, :] = jnp.where(lane_ids == index, inverse, rs[rows, :])

    def kept_inverse(index, rows):
        return jnp.sum(jnp.where(lane_ids == index, rs[rows, :], 0.0), axis=-1, keepdims=True)

    piece_rows = features // shards // 4
    far = len(far_peers)
    AT_Z, AT_FAR, AT_BACK, AT_CORE = 2, 2 + len(turns), 2 + len(turns) + far, 3 + len(turns) + far
    FREE_Z, FREE_FAR = 2, 3
    trio = 3 * LANES
    half = hidden // 2
    group = [0, 1, 2, 3, 3, 4, 4, 5, 6, 6, 6, 6]
    unit_set = [(0, 1, 0, 1, 0, 1, 0)[g] for g in group]
    first_set = [(0, 1, 2, 0, 1, 2, 0)[g] for g in group]
    halves = [slice(0, half), slice(half, hidden)]
    unit_cols = [slice(0, hidden)] * 3 + halves + halves + [slice(0, hidden)] + [
        slice(3 * width, hidden), slice(0, 2 * trio), slice(2 * trio, 3 * trio), slice(3 * trio, 4 * trio)
    ]
    unit_far_first = [g in (1, 4) for g in group]
    unit_at = [(4, 6, 2, 3, 5, other, own)[g] for g in group]
    opens = [u == 0 or group[u] != group[u - 1] for u in range(UNITS)]
    closes = [u + 1 == UNITS or group[u] != group[u + 1] for u in range(UNITS)]
    LAST_WHOLE = 7
    parts_of_own = [8, 9, 10, 11]

    def first_bit(unit):
        return role if unit_far_first[unit] else side

    def first_peer(unit):
        return half_peer if unit_far_first[unit] else side_peer

    def far_list(unit):
        return [side_peer] + far_peers[:-1] if unit_far_first[unit] else far_peers

    def reduce_copy(unit, stage, src, dst, peer):
        return pltpu.make_async_remote_copy(
            src_ref=src, dst_ref=dst, send_sem=rs_send.at[unit, stage], recv_sem=rs_recv.at[unit, stage],
            device_id=peer, device_id_type=MESH,
        )

    def rows_of(first, count):
        return pl.ds(pl.multiple_of(first * piece_rows, piece_rows), count * piece_rows)

    def copy_core(unit):
        where, cols = unit_set[unit], unit_cols[unit]
        src = gs.at[where, :, rows_of(2 - 2 * core, 2), cols]
        return reduce_copy(unit, 0, src, r0.at[where, :, :, cols], core_peer)

    def copy_first(unit):
        where, cols = unit_set[unit], unit_cols[unit]
        src = r0.at[where, :, rows_of(1 - first_bit(unit), 1), cols]
        return reduce_copy(unit, 1, src, r1.at[first_set[unit], :, :, cols], first_peer(unit))

    def copy_z(unit, k):
        where, cols = unit_set[unit], unit_cols[unit]
        return reduce_copy(
            unit, AT_Z + k - 1, r1.at[first_set[unit], later(k), :, cols], r2.at[where, k - 1, :, cols],
            (section, later(k)),
        )

    def crosses(unit, b):
        return unit >= LAST_WHOLE and b == far - 1

    def copy_far(unit, b):
        where, cols = unit_set[unit], unit_cols[unit]
        there = 1 - where if crosses(unit, b) else where
        return reduce_copy(
            unit, AT_FAR + b, r3s.at[where, :, cols], r3r.at[there, b, :, cols], far_list(unit)[b]
        )

    def spend(unit, kind, where, count=1):
        if opens[unit] and group[unit] >= (3 if kind == 1 else 2):
            pl.semaphore_wait(free.at[kind, where], count)

    def gain(unit, kind, peers_of):
        after = group[unit] + (3 if kind == 1 else 2)
        if closes[unit] and after in group:
            where = (first_set if kind == 1 else unit_set)[unit]
            for peer in peers_of(group.index(after)):
                pl.semaphore_signal(free.at[kind, where], inc=1, device_id=peer, device_id_type=MESH)

    def start_far(unit, b):
        where = unit_set[unit]
        spend(unit, FREE_FAR + b, 1 - where if crosses(unit, b) else where)
        copy_far(unit, b).start()

    def take_far(unit, b):
        if not crosses(unit, b):
            copy_far(unit, b).wait_recv()
        elif unit == LAST_WHOLE:
            for part in parts_of_own:
                cols = unit_cols[part]
                arrived = r3r.at[1, b, :, cols]
                reduce_copy(part, AT_FAR + b, arrived, arrived, half_peer).wait_recv()
        elif unit == parts_of_own[0]:
            arrived = r3r.at[0, b]
            reduce_copy(LAST_WHOLE, AT_FAR + b, arrived, arrived, half_peer).wait_recv()

    def out_rows(unit, first, count):
        return gout.at[unit_at[unit], rows_of(first, count), unit_cols[unit]]

    def copy_back(unit):
        mine = 2 * core + first_bit(unit)
        src = r3s.at[unit_set[unit], :, unit_cols[unit]]
        return reduce_copy(unit, AT_BACK, src, out_rows(unit, mine, 1), first_peer(unit))

    def copy_keep(unit):
        mine = 2 * core + first_bit(unit)
        src = r3s.at[unit_set[unit], :, unit_cols[unit]]
        return pltpu.make_async_copy(src, out_rows(unit, mine, 1), rs_keep.at[unit])

    def copy_back_core(unit):
        rows = out_rows(unit, 2 * core, 2)
        return reduce_copy(unit, AT_CORE, rows, rows, core_peer)

    def sum_start(unit):
        spend(unit, 0, unit_set[unit])
        copy_core(unit).start()

    def sum_core(unit):
        where, cols = unit_set[unit], unit_cols[unit]
        copy_core(unit).wait()

        def add(block, carry):
            mine = gs[where, block, rows_of(2 * core, 2), cols].astype(F32)
            r0[where, block, :, cols] = (r0[where, block, :, cols].astype(F32) + mine).astype(BF)
            return carry

        lax.fori_loop(0, shards, add, 0)
        spend(unit, 1, first_set[unit])
        copy_first(unit).start()

    def sum_first(unit):
        where, cols = unit_set[unit], unit_cols[unit]
        copy_first(unit).wait()

        def add(block, carry):
            mine = r0[where, block, rows_of(first_bit(unit), 1), cols].astype(F32)
            held = r1[first_set[unit], block, :, cols].astype(F32)
            r1[first_set[unit], block, :, cols] = (held + mine).astype(BF)
            return carry

        lax.fori_loop(0, shards, add, 0)
        gain(unit, 0, lambda following: [core_peer])
        spend(unit, FREE_Z, where, len(turns))
        for k in turns:
            copy_z(unit, k).start()

    def sum_z(unit):
        where, cols = unit_set[unit], unit_cols[unit]
        for k in turns:
            copy_z(unit, k).wait()
        total = r1[first_set[unit], shard, :, cols].astype(F32)
        for k in turns:
            total += r2[where, k - 1, :, cols].astype(F32)
        r3s[where, :, cols] = total.astype(BF)
        gain(unit, 1, lambda following: [first_peer(following)])
        gain(unit, FREE_Z, lambda following: [(section, later(k)) for k in turns])
        start_far(unit, 0)

    def sum_far(unit):
        where, cols = unit_set[unit], unit_cols[unit]
        for b in range(far):
            copy_far(unit, b).wait_send()
            take_far(unit, b)
            total = r3s[where, :, cols].astype(F32) + r3r[where, b, :, cols].astype(F32)
            r3s[where, :, cols] = total.astype(BF)
            gain(unit, FREE_FAR + b, lambda following, b=b: [far_list(following)[b]])
            if b + 1 < far:
                start_far(unit, b + 1)
        copy_keep(unit).start()
        copy_back(unit).start()

    def sum_back(unit):
        copy_keep(unit).wait()
        copy_back(unit).wait_send()
        arrived = out_rows(unit, 2 * core + 1 - first_bit(unit), 1)
        reduce_copy(unit, AT_BACK, arrived, arrived, first_peer(unit)).wait_recv()
        copy_back_core(unit).start()

    def sum_end(unit):
        copy_back_core(unit).wait_send()
        arrived = out_rows(unit, 2 - 2 * core, 2)
        reduce_copy(unit, AT_CORE, arrived, arrived, core_peer).wait_recv()

    small_peers = far_peers + [side_peer]

    def copy_small(b):
        at = len(turns) + b
        return pltpu.make_async_remote_copy(
            src_ref=sg.at[shard], dst_ref=sgz.at[at], send_sem=sg_send.at[at],
            recv_sem=sg_recv.at[at], device_id=small_peers[b], device_id_type=MESH,
        )

    def copy_small_core():
        at = len(turns) + len(small_peers)
        return pltpu.make_async_remote_copy(
            src_ref=sg, dst_ref=sgr, send_sem=sg_send.at[at],
            recv_sem=sg_recv.at[at], device_id=core_peer, device_id_type=MESH,
        )

    def copy_small_z(k):
        return pltpu.make_async_remote_copy(
            src_ref=sg.at[later(k)], dst_ref=sgz.at[k - 1], send_sem=sg_send.at[k - 1],
            recv_sem=sg_recv.at[k - 1], device_id=(section, later(k)), device_id_type=MESH,
        )

    def small_start():
        for owner in range(shards):
            cols = slice(owner * LANES, (owner + 1) * LANES)
            rows = [gacc[row, :, cols] for row in range(MASK_ROW + 1)]
            rest = jnp.zeros((SMALL_ROWS - MASK_ROW - 1, LANES), F32)
            sg[owner] = jnp.concatenate(rows + [rest], axis=0) + pick[...] * gacc[STEP_ROW, :, cols]
        copy_small_core().start()

    def small_core():
        copy_small_core().wait()
        sg[...] += sgr[...]
        for k in turns:
            copy_small_z(k).start()

    def small_z():
        for k in turns:
            copy_small_z(k).wait()
        sg[shard] += sum(sgz[k - 1] for k in turns)
        copy_small(0).start()

    def small_add(b):
        copy_small(b).wait()
        sg[shard] += sgz[len(turns) + b]
        if b + 1 < len(small_peers):
            copy_small(b + 1).start()
        else:
            gv[...] = sg[shard]

    def embed(layer):
        flag = layer.astype(F32)

        def body(rows):
            source = x[layer, rows, :].astype(F32)
            masked = rs[rows, MASK_LANE : MASK_LANE + 1] * flag > 0.5
            value = jnp.where(masked, vec[MASK_ROW], source) + vec[STEP_ROW] * flag
            res[layer, rows, :] = value
            x[layer, rows, :] = value.astype(BF)

        for_rows(body)

    def project(source, weight, target, first, last):
        for c in range(first, last):
            cols = slice(c * width, (c + 1) * width)

            def body(rows, cols=cols):
                target[rows, cols] = dot(source[rows, :], weight[:, cols]).astype(BF)

            for_rows(body)

    queries = length // AB

    def attend(which, polls=()):
        source, target, saved = qkv.at[which], oa.at[which], p_hbm.at[which]
        steps = pairs * queries

        def store(t):
            slot = lax.rem(t, 2)
            return pltpu.make_async_copy(big.at[pl.ds(2 * slot, 2)], saved.at[t], big_sem.at[slot])

        def step(t, carry):
            hp, qb = t // queries, lax.rem(t, queries)
            slot = lax.rem(t, 2)
            rows = rows_at(qb, AB)
            q = source[rows, lanes_at(hp)] * jnp.asarray(0.125, BF)
            k = source[:, lanes_at(pairs + hp)]
            v = source[:, lanes_at(2 * pairs + hp)]

            @pl.when(t >= 2)
            def _():
                store(t - 2).wait()

            for when, act in polls:
                pl.when(t == when)(act)

            low = low_half((AB, LANES))
            zero = jnp.zeros_like(q)
            scores = [dot(jnp.where(low if j == 0 else ~low, q, zero), k, NT) for j in range(2)]
            parts = []
            for j in range(2):
                e = jnp.exp(scores[j] - jnp.max(scores[j], axis=-1, keepdims=True))
                weights = (e * (1.0 / jnp.sum(e, axis=-1, keepdims=True))).astype(BF)
                for h in range(2):
                    big[2 * slot + j, h * AB : (h + 1) * AB, :] = weights[:, h * width : (h + 1) * width]
                parts.append(dot(weights, v))
            target[rows, lanes_at(hp)] = jnp.where(low, parts[0], parts[1]).astype(BF)
            store(t).start()
            return carry

        lax.fori_loop(0, steps, step, 0)
        for t in range(steps - 2, steps):
            store(t).wait()

    def out_norm(which, res_at, xh_at, gain_row, shift_row, hb_at):
        def body(rows):
            value = dot(oa[which, rows, :], wa[which, :, 3 * width :]) + res[res_at, rows, :]
            normal, inverse = norm_rows(value)
            result = normal * vec[gain_row] + vec[shift_row]
            xh[xh_at, rows, :] = normal.astype(BF)
            keep_inverse(xh_at, rows, inverse)
            res[res_at, rows, :] = result
            hb[hb_at, rows, :] = result.astype(BF)

        for_rows(body)

    chunks = hidden // width

    def up_chunk(layer, c):
        starts = [z * width + c * block_rows for z in range(shards)]
        return jnp.concatenate([wu[layer, :, i : i + block_rows] for i in starts], axis=1)

    def down_chunk(layer, c):
        starts = [z * width + c * block_rows for z in range(shards)]
        return jnp.concatenate([wd[layer, i : i + block_rows, :] for i in starts], axis=0)

    def feed_store(layer, c):
        slot = c % 2
        return pltpu.make_async_copy(big.at[2 * slot : 2 * slot + 2], f_hbm.at[layer, c], big_sem.at[slot])

    def feed_load(layer, c):
        slot = c % 2
        return pltpu.make_async_copy(f_hbm.at[layer, c], big.at[2 * slot : 2 * slot + 2], big_sem.at[slot])

    def feed(layer, hb_at, polls=()):
        for c in range(chunks):
            slot = c % 2
            cols = slice(c * width, (c + 1) * width)
            if c >= 2:
                feed_store(layer, c - 2).wait()

            parts = [slice(r * RB, (r + 1) * RB) for r in range(length // RB)]
            lifted = [dot(hb[hb_at, parts[0], :], up_chunk(layer, c))]
            for r, rows in enumerate(parts):
                if r + 1 < len(parts):
                    lifted.append(dot(hb[hb_at, parts[r + 1], :], up_chunk(layer, c)))
                value, slope = gelu_both(lifted[r])
                value = value.astype(BF)
                big[2 * slot, rows, :] = value
                big[2 * slot + 1, rows, :] = slope.astype(BF)
                res[layer, rows, :] += dot(value, down_chunk(layer, c))

            feed_store(layer, c).start()
            for when, act in polls:
                if when == c:
                    act()
        for c in range(chunks - 2, chunks):
            feed_store(layer, c).wait()

    def final_norm(layer, xh_at, gain_row, shift_row, target, kept=None):
        kept = xh.at[xh_at] if kept is None else kept

        def body(rows):
            normal, inverse = norm_rows(res[layer, rows, :])
            kept[rows, :] = normal.astype(BF)
            keep_inverse(xh_at, rows, inverse)
            target[rows, :] = (normal * vec[gain_row] + vec[shift_row]).astype(BF)

        for_rows(body)

    def norm_back(load, res_at, xh_at, gain_row, shift_row, kept=None):
        kept = xh.at[xh_at] if kept is None else kept

        def body(rows):
            upstream = load(rows)
            normal = kept[rows, :].astype(F32)
            result = norm_rows_back(upstream, normal, kept_inverse(xh_at, rows), vec[gain_row])
            gacc[gain_row] += jnp.sum(upstream * normal, axis=0, keepdims=True)
            gacc[shift_row] += jnp.sum(upstream, axis=0, keepdims=True)
            res[res_at, rows, :] = result
            dfb[rows, :] = result.astype(BF)

        for_rows(body)

    def feed_back(layer, hb_at, up, down, polls=()):
        feed_load(layer, 0).start()
        feed_load(layer, 1).start()
        for c in range(chunks):
            slot = c % 2
            cols = slice(c * width, (c + 1) * width)
            feed_load(layer, c).wait()

            parts = [slice(r * RB, (r + 1) * RB) for r in range(length // RB)]
            grads = [dot(dfb[parts[0], :], down_chunk(layer, c), NT)]
            for r, rows in enumerate(parts):
                if r + 1 < len(parts):
                    grads.append(dot(dfb[parts[r + 1], :], down_chunk(layer, c), NT))
                grad = (grads[r] * big[2 * slot + 1, rows, :].astype(F32)).astype(BF)
                dp[rows, :] = grad
                res[layer, rows, :] += dot(grad, up_chunk(layer, c), NT)
            by_owner(up, cols, dot(hb[hb_at], dp[...], TN))
            by_owner(down, cols, dot(big[2 * slot], dfb[...], TN))
            if c + 2 < chunks:
                feed_load(layer, c + 2).start()
            for when, act in polls:
                if when == c:
                    act()

    def by_owner(target, cols, value):
        target[:, :, cols] = value.astype(BF).reshape(shards, features // shards, -1)

    def attend_back(which, polls=()):
        source, output, saved = qkv.at[which], oa.at[which], p_hbm.at[which]
        steps = pairs * queries

        def fetch(t):
            slot = lax.rem(t, 2)
            return pltpu.make_async_copy(saved.at[t], big.at[pl.ds(2 * slot, 2)], big_sem.at[slot])

        fetch(0).start()

        def step(t, carry):
            hp, qb = t // queries, lax.rem(t, queries)
            slot = lax.rem(t, 2)
            rows = rows_at(qb, AB)

            @pl.when(t + 1 < steps)
            def _():
                fetch(t + 1).start()

            for when, act in polls:
                pl.when(t == when)(act)

            fetch(t).wait()

            @pl.when(qb == 0)
            def _():
                kvt[...] = jnp.zeros_like(kvt)

            q = source[rows, lanes_at(hp)]
            k = source[:, lanes_at(pairs + hp)]
            v = source[:, lanes_at(2 * pairs + hp)]
            do = dob[rows, lanes_at(hp)]
            inner = do.astype(F32) * output[rows, lanes_at(hp)].astype(F32)
            low = low_half((AB, LANES))
            zero = jnp.zeros_like(q)
            parts = []
            for j in range(2):
                mine = low if j == 0 else ~low
                dom = jnp.where(mine, do, zero)
                delta = jnp.sum(jnp.where(mine, inner, 0.0), axis=-1, keepdims=True)
                weights = jnp.concatenate(
                    [big[2 * slot + j, h * AB : (h + 1) * AB, :] for h in range(2)], axis=1
                )
                ds = (weights.astype(F32) * (dot(dom, v, NT) - delta)).astype(BF)
                kvt[1] += dot(dom, weights, TN)
                kvt[0] += dot(jnp.where(mine, q, zero), ds, TN)
                parts.append(dot(ds, k))
            source[rows, lanes_at(hp)] = (jnp.where(low, parts[0], parts[1]) * 0.125).astype(BF)

            @pl.when(qb == queries - 1)
            def _():
                source[:, lanes_at(pairs + hp)] = jnp.transpose(kvt[0] * 0.125).astype(BF)
                source[:, lanes_at(2 * pairs + hp)] = jnp.transpose(kvt[1]).astype(BF)

            return carry

        lax.fori_loop(0, steps, step, 0)

    def grad_weight(target, first, last, left, which):
        for c in range(first, last):
            cols = slice(c * width, (c + 1) * width)
            by_owner(target, cols, dot(left[...], qkv[which, :, cols], TN))

    def grad_trio(target, left, which, hp):
        blocks_of = [qkv[which, :, lanes_at(n * pairs + hp)] for n in range(3)]
        value = dot(left[...], jnp.concatenate(blocks_of, axis=1), TN)
        by_owner(target, slice(hp * trio, (hp + 1) * trio), value)

    def out_grad(which, target):
        by_owner(target, slice(3 * width, 4 * width), dot(oa[which], dfb[...], TN))

    def out_back(which):

        def body(rows):
            dob[rows, :] = dot(dfb[rows, :], wa[which, :, 3 * width :], NT).astype(BF)

        for_rows(body)

    barrier = pltpu.get_barrier_semaphore()
    peers = [(section, later(k)) for k in turns] + [core_peer, side_peer] + far_peers
    for peer in peers:
        pl.semaphore_signal(barrier, inc=1, device_id=peer, device_id_type=MESH)
    for unit in range(5):
        load_masters(unit)
    load_x = pltpu.make_async_copy(x_in.at[own], x.at[own], cot_sem.at[0])
    load_x.start()
    gacc[...] = jnp.zeros_like(gacc)

    rows = [enc_gains[...], enc_shifts[...], dec_gains[...], dec_shifts[...], mask_embed[...], time_table[...]]
    count = sum(row.shape[0] for row in rows)
    rows.append(jnp.zeros((SMALL_ROWS - count, LANES), F32))
    small[shard] = jnp.concatenate(rows, axis=0).astype(BF)
    pair_row = ((section - (sections // 2) * role) * shards + shard) * 2 + role
    row_ids = lax.broadcasted_iota(jnp.int32, (SMALL_ROWS, LANES), 0)
    pick[...] = (row_ids == MASK_ROW + 1 + timestep[pair_row]).astype(F32)
    round_layer(own)
    pl.semaphore_wait(barrier, len(peers))

    for k in turns:
        small_copy(k).start()
    for item in range(4):
        send(item, 0)
    swap_x = swap_copy(x_in.at[other], x.at[own], 0)
    swap_x.start()
    round_layer(other)
    send(4, 0)
    load_masters(5)
    load_masters(6)
    round_master(2, wu, 0)
    send(5, 0)
    round_master(3, wd, 0, True)
    send(6, 0)
    round_master(4, wa, 2)
    send(7, 0)
    round_master(5, wu, 1)
    send(8, 0)
    round_master(6, wd, 1, True)
    send(9, 0)
    swap_cot = swap_copy(cot_in.at[other], cot_land, 1)
    swap_cot.start()

    batch = marks.shape[1]
    total_rows = route.shape[0]
    mine = jnp.zeros((2, length), F32)
    tally = jnp.zeros((1, 1), F32)
    for first in range(0, total_rows, batch):
        for n, array in enumerate((route, remask)):
            copy = pltpu.make_async_copy(array.at[first : first + batch, :], marks.at[n], lo_sem.at[n])
            copy.start()
            copy.wait()
        ids = lax.broadcasted_iota(jnp.int32, (batch, length), 0) + first
        routed = marks[0].astype(F32)
        same = jnp.where(lax.rem(ids, 2) == role, routed, 0.0)
        tally += jnp.sum(jnp.sum(same, axis=0, keepdims=True), axis=1, keepdims=True)
        picked = [
            jnp.sum(jnp.where(ids == pair_row, value, 0.0), axis=0, keepdims=True)
            for value in (marks[1].astype(F32), routed)
        ]
        mine += jnp.concatenate(picked, axis=0)
    scale = mine[1:2, :] * float(total_rows // 2 * length) / tally
    wide_ids = lax.broadcasted_iota(jnp.int32, (LANES, length), 0)
    wide = jnp.where(wide_ids == MASK_LANE, mine[0:1, :], jnp.where(wide_ids == SCALE_LANE, scale, 0.0))
    rs[...] = jnp.transpose(wide)

    for k in turns:
        small_copy(k).wait_recv()
    for owner in range(shards):
        values = small[owner].astype(F32)
        cols = slice(owner * LANES, (owner + 1) * LANES)
        for row in range(MASK_ROW + 1):
            vec[row, :, cols] = values[row : row + 1, :]
        vec[STEP_ROW, :, cols] = jnp.sum(values * pick[...], axis=0, keepdims=True)
    load_x.wait()
    embed(own)

    def pass_side(item):
        take(item, 0)
        send(item, 1)

    def pass_core(item):
        take(item, 1)
        send(item, 2)

    def ready(item):
        take(item, 2)

    def polls_of(*acts):
        return [(when, functools.partial(act, item)) for when, act, item in acts]

    pass_side(0)
    pass_side(1)
    pass_core(0)
    pass_side(2)
    pass_core(1)
    for c in range(3):
        ready(c)
        project(x.at[own], wa.at[own], qkv.at[own], c, c + 1)
        if c == 0:
            pass_core(2)
            pass_side(3)
    attend(own, polls_of((2, pass_core, 3), (4, pass_side, 4)))
    ready(3)
    pass_core(4)
    out_norm(own, own, own, 4 * own, 2 + 5 * own, own)
    swap_copy(x_in.at[other], x.at[other], 0).wait_recv()
    pass_side(5)
    embed(other)
    ready(4)
    project(x.at[other], wa.at[other], qkv.at[other], 0, 3)
    attend(other, polls_of((4, pass_core, 5), (4, pass_side, 6), (7, pass_side, 7)))
    pass_core(6)
    out_norm(other, other, other, 4 * other, 2 + 5 * other, other)
    ready(5)
    h_store = pltpu.make_async_copy(hb.at[0], h_land, h_sem)
    h_load = pltpu.make_async_copy(h_land, hb.at[0], h_sem)
    h_store.start()
    ready(6)
    feed(0, 0, polls_of((3, pass_core, 7), (3, pass_side, 8)))
    h_store.wait()
    final_norm(0, 2, 1, 3, hb.at[2])
    keep_memory = pltpu.make_async_copy(hb.at[2], lo.at[own], lo_sem.at[0])
    pl.when(role == 0)(keep_memory.start)
    for i in range(QUARTERS):
        pl.when(role == 1)(send_lo(hb.at[2], i).start)
    ready(7)
    project(hb.at[1], wa.at[2], qkv.at[2], 0, 1)
    project(hb.at[2], wa.at[2], qkv.at[2], 1, 3)
    attend(2, polls_of((4, pass_core, 8), (4, pass_side, 9)))
    pass_core(9)
    out_norm(2, 1, 3, 5, 8, 0)
    ready(8)
    ready(9)
    def load_cot(layer):
        here = pltpu.make_async_copy(cot_in.at[own], dp, cot_sem.at[1])
        there = pltpu.make_async_copy(cot_land, dp, cot_sem.at[1])
        pl.when(own == layer)(here.start)
        pl.when(own != layer)(there.start)
        return here

    swap_copy(cot_in.at[other], cot_land, 1).wait_recv()
    load_result_cot = load_cot(1)
    feed(1, 0)
    final_norm(1, 4, 6, 9, dob, big.at[3])
    keep_result = pltpu.make_async_copy(dob, lo.at[own], lo_sem.at[0])
    stage_result = pltpu.make_async_copy(dob, out_land, lo_sem.at[1])
    pl.when(role == 1)(keep_result.start)
    stage_result.start()

    def result_upstream(rows):
        return dp[rows, :].astype(F32) * rs[rows, SCALE_LANE : SCALE_LANE + 1]

    load_result_cot.wait()
    norm_back(result_upstream, 1, 4, 6, 9, big.at[3])
    stage_result.wait()
    keep_result.wait()
    feed_back(1, 0, gs.at[0], gs.at[1])
    h_load.start()
    load_memory_cot = load_cot(0)
    sum_start(0)
    sum_start(1)
    norm_back(lambda rows: res[1, rows, :], 1, 3, 5, 8)
    out_back(2)

    def lo_part(i):
        pl.when(role == 0)(send_lo(out_land, i).start)

    attend_back(
        2,
        polls_of((1, sum_core, 0), (1, sum_core, 1), (6, sum_first, 0), (6, sum_first, 1), (6, lo_part, 0)),
    )
    out_grad(2, gs.at[0])
    grad_weight(gs.at[0], 0, 1, hb.at[1], 2)
    grad_weight(gs.at[0], 1, 3, hb.at[2], 2)
    sum_start(2)
    load_memory_cot.wait()

    def cross_body(rows):
        res[1, rows, :] += dot(qkv[2, rows, :width], wa[2, :, :width], NT)
        res[0, rows, :] = dp[rows, :].astype(F32) + dot(
            qkv[2, rows, width:], wa[2, :, width : 3 * width], NT
        )

    for_rows(cross_body)
    sum_core(2)
    norm_back(lambda rows: res[0, rows, :], 0, 2, 1, 3)
    sum_z(0)
    h_load.wait()
    feed_back(
        0, 0, gs.at[1], gs.at[0],
        polls_of(
            (0, sum_far, 0), (0, lo_part, 1), (1, sum_start, 3), (2, sum_first, 2), (2, sum_start, 5),
            (2, sum_z, 1), (2, sum_core, 3), (2, sum_back, 0), (3, sum_core, 5), (3, sum_far, 1),
            (3, sum_end, 0),
        ),
    )
    sum_start(4)
    sum_start(6)

    def gin_part(i):
        send_gin(i).start()

    for turn, layer in enumerate((other, own)):
        slot = 1 - turn
        flag = layer.astype(F32)
        source = x.at[layer]
        target = gs.at[slot]
        norm_back(lambda rows: res[layer, rows, :], layer, layer, 4 * layer, 2 + 5 * layer)
        out_back(layer)

        def last_part(unit):
            for hp in {9: (0, 1), 10: (2,), 11: (3,)}[unit]:
                grad_trio(target, source, layer, hp)
            sum_start(unit)

        if turn == 0:
            acts = polls_of(
                (1, sum_z, 2), (1, sum_core, 4), (1, sum_core, 6), (2, sum_first, 3), (2, sum_back, 1),
                (2, sum_first, 5), (3, sum_end, 1), (3, sum_far, 2), (4, sum_first, 4), (5, sum_first, 6),
                (5, sum_back, 2), (5, sum_z, 3), (6, sum_end, 2), (6, lo_part, 2), (7, sum_z, 5),
                (7, sum_far, 3),
            )
        else:
            out_grad(layer, target)
            sum_start(8)
            acts = polls_of(
                (0, sum_far, 5), (0, sum_z, 6), (0, sum_far, 4), (1, sum_core, 8), (1, lo_part, 3),
                (1, sum_back, 5), (2, sum_first, 7), (2, sum_far, 6), (2, sum_back, 4), (3, gin_part, 1),
                (3, sum_end, 5), (4, last_part, 9), (4, sum_first, 8), (4, sum_end, 4),
                (4, gin_part, 2), (5, sum_core, 9), (5, sum_back, 6), (6, last_part, 10), (6, sum_end, 6),
                (6, gin_part, 3), (7, sum_core, 10), (7, sum_z, 7), (7, sum_first, 9),
            )
        attend_back(layer, acts)
        if turn == 0:
            sum_z(4)
            out_grad(layer, target)
            for hp in range(pairs):
                grad_trio(target, source, layer, hp)
            sum_start(7)
            sum_back(3)
        else:
            last_part(11)
            sum_first(10)
            sum_z(8)

        def body(rows):
            value = res[layer, rows, :] + dot(qkv[layer, rows, :], wa[layer, :, : 3 * width], NT)
            masked = rs[rows, MASK_LANE : MASK_LANE + 1] * flag > 0.5
            gacc[MASK_ROW] += jnp.sum(jnp.where(masked, value, 0.0), axis=0, keepdims=True)
            gacc[STEP_ROW] += jnp.sum(value, axis=0, keepdims=True) * flag
            value = jnp.where(masked, 0.0, value)
            res[layer, rows, :] = value
            if turn == 0:
                dp[rows, :] = value.astype(BF)

        for_rows(body)
        if turn == 0:
            sum_core(7)
            sum_end(3)
            gin_part(0)
        else:
            keep_gin = pltpu.make_async_copy(res.at[layer], gin.at[layer], gin_sem.at[0])
            keep_gin.start()
    sum_core(11)
    small_start()
    sum_far(8)
    sum_z(9)
    small_core()
    for i in range(QUARTERS):
        send_gin(i).wait()
    load_gin = pltpu.make_async_copy(gin_land, dob, gin_sem.at[1])
    load_gin.start()
    load_gin.wait()

    def widen(rows):
        res[other, rows, :] = dob[rows, :].astype(F32)

    for_rows(widen)
    keep_other = pltpu.make_async_copy(res.at[other], gin.at[other], gin_sem.at[1])
    keep_other.start()
    sum_first(11)
    sum_z(10)
    sum_far(9)
    small_z()
    sum_z(11)
    sum_far(10)
    for b in range(far):
        small_add(b)
    sum_far(11)
    sum_far(7)
    for unit in (8, 9, 10, 11):
        sum_back(unit)
    small_add(far)
    sum_back(7)
    for unit in (8, 9, 10, 11, 7):
        sum_end(unit)
    keep_other.wait()
    keep_gin.wait()
    for i in range(QUARTERS):
        send_lo(out_land, i).wait()
    swap_x.wait_send()
    swap_cot.wait_send()
    for k in turns:
        small_copy(k).wait_send()
    for item in range(len(items)):
        for stage in range(3):
            for k in turns:
                src, dst, peer = hop(item, stage, k)
                remote(src, dst, (item, stage, k - 1), peer).wait_send()


def run_pair(tokens, cotangent, route, remask, timestep, masters, small):
    _, length, features = tokens.shape
    shards = lax.axis_size("shard")
    hidden = masters[2].shape[1]
    pairs = features // LANES
    quarters = features // shards
    far = (lax.axis_size("section") // 4).bit_length() - 1
    hbm = pl.BlockSpec(memory_space=pl.ANY)
    vmem = pl.BlockSpec(memory_space=pltpu.VMEM)
    smem = pl.BlockSpec(memory_space=pltpu.SMEM)
    dma = pltpu.SemaphoreType.DMA
    full_a = (3, features, 4 * features)
    full_u = (2, features, hidden)
    full_d = (2, hidden, features)
    out = jax.ShapeDtypeStruct
    one = out(tokens.shape[1:], BF)
    return pl.pallas_call(
        kernel,
        name="pair",
        out_shape=[
            out(tokens.shape, BF),
            out(tokens.shape, F32),
            out((OWNED, features // shards, 4 * features), BF),
            out((SMALL_ROWS, LANES), F32),
            out((3, pairs * (length // AB), 2, length, features), BF),
            out((2, hidden // features, 2, length, features), BF),
            one, one, one, one,
        ],
        in_specs=[hbm] * 4 + [smem] + [hbm] * len(masters) + [vmem] * len(small),
        out_specs=[hbm] * 3 + [vmem] + [hbm] * 6,
        scratch_shapes=[
            pltpu.VMEM(full_a, BF),
            pltpu.VMEM(full_u, BF),
            pltpu.VMEM(full_d, BF),
            pltpu.VMEM((shards, SMALL_ROWS, LANES), BF),
            pltpu.VMEM((VEC_ROWS, 1, features), F32),
            pltpu.VMEM((SMALL_ROWS, LANES), F32),
            pltpu.VMEM((2, min(32, route.shape[0]), length), jnp.int32),
            pltpu.VMEM((VEC_ROWS, 1, features), F32),
            pltpu.VMEM((2, length, features), BF),
            pltpu.VMEM((3, length, 3 * features), BF),
            pltpu.VMEM((3, length, features), BF),
            pltpu.VMEM((4, length, features), BF),
            pltpu.VMEM((length, LANES), F32),
            pltpu.VMEM((3, length, features), BF),
            pltpu.VMEM((2, length, features), F32),
            pltpu.VMEM((length, features), BF),
            pltpu.VMEM((length, features), BF),
            pltpu.VMEM((4, length, features), BF),
            pltpu.VMEM((length, features), BF),
            pltpu.VMEM((2, LANES, length), F32),
            pltpu.VMEM((2, shards, quarters, hidden), BF),
            pltpu.VMEM((2, shards, quarters // 2, hidden), BF),
            pltpu.VMEM((3, shards, quarters // 4, hidden), BF),
            pltpu.VMEM((2, shards - 1, quarters // 4, hidden), BF),
            pltpu.VMEM((2, quarters // 4, hidden), BF),
            pltpu.VMEM((2, far, quarters // 4, hidden), BF),
            pltpu.VMEM((shards, SMALL_ROWS, LANES), F32),
            pltpu.VMEM((shards, SMALL_ROWS, LANES), F32),
            pltpu.VMEM((shards + far, SMALL_ROWS, LANES), F32),
            dma((ITEMS, 3, shards - 1)),
            dma((ITEMS, 3, shards - 1)),
            dma((OWNED, 4)),
            dma((3, shards - 1)),
            dma((2, 10)),
            dma((2,)),
            dma,
            dma((4,)),
            dma((2,)),
            dma((2,)),
            dma((UNITS, 3 + shards + far)),
            dma((UNITS, 3 + shards + far)),
            dma((UNITS,)),
            dma((shards + 1 + far,)),
            dma((shards + 1 + far,)),
            pltpu.SemaphoreType.REGULAR((3 + far, 3)),
        ],
        compiler_params=pltpu.CompilerParams(
            vmem_limit_bytes=64 << 20, has_side_effects=True, collective_id=0
        ),
    )(tokens, cotangent, route, remask, timestep, *masters, *small)


def finish_kernel(
    gout, gv,
    enc_qkv, enc_out, enc_up, enc_down, enc_gains, enc_shifts,
    dec_qkv, dec_out, cross_query, cross_kv, cross_out, dec_up, dec_down, dec_gains, dec_shifts,
    time_table, mask_embed,
):
    width = enc_out.shape[1]
    pairs = width // LANES
    for unit, qkv, out in ((0, enc_qkv, enc_out), (1, dec_qkv, dec_out)):
        for hp in range(pairs):
            for n in range(3):
                to, at = (n * pairs + hp) * LANES, (hp * 3 + n) * LANES
                qkv[:, to : to + LANES] = gout[unit, :, at : at + LANES].astype(F32)
        out[...] = gout[unit, :, 3 * width :].astype(F32)
    cross_query[...] = gout[2, :, :width].astype(F32)
    cross_kv[...] = gout[2, :, width : 3 * width].astype(F32)
    cross_out[...] = gout[2, :, 3 * width :].astype(F32)
    count = gout.shape[1]
    owners = width // count
    for unit, up in ((3, enc_up), (4, dec_up)):
        for c in range(owners):
            for z in range(owners):
                to, at = z * width + c * count, c * width + z * count
                up[:, to : to + count] = gout[unit, :, at : at + count].astype(F32)
    for unit, down in ((5, enc_down), (6, dec_down)):
        for j in range(down.shape[0] // count):
            down[j * count : (j + 1) * count, :] = gout[unit, :, j * width : (j + 1) * width].astype(F32)
    enc_gains[...] = gv[0:2, :]
    enc_shifts[...] = gv[2:4, :]
    dec_gains[...] = gv[4:7, :]
    dec_shifts[...] = gv[7:10, :]
    mask_embed[...] = gv[MASK_ROW : MASK_ROW + 1, :]
    time_table[...] = gv[MASK_ROW + 1 : MASK_ROW + 1 + time_table.shape[0], :]


def per_device(
    tokens, cotangent, route, remask, timestep,
    enc_qkv, enc_out, enc_up, enc_down, enc_gains, enc_shifts,
    dec_qkv, dec_out, cross_query, cross_kv, cross_out, dec_up, dec_down, dec_gains, dec_shifts,
    time_table, mask_embed,
):
    masters = (
        enc_qkv, enc_out, enc_up, enc_down, dec_qkv, dec_out,
        cross_query, cross_kv, cross_out, dec_up, dec_down,
    )
    mask_row = mask_embed[None, :]
    small = (enc_gains, enc_shifts, dec_gains, dec_shifts, mask_row, time_table)
    layer_out, grad_in, gout, gv = run_pair(
        tokens, cotangent, route, remask, timestep, masters, small
    )[:4]
    owned = (
        enc_qkv, enc_out, enc_up, enc_down, enc_gains, enc_shifts,
        dec_qkv, dec_out, cross_query, cross_kv, cross_out, dec_up, dec_down, dec_gains, dec_shifts,
        time_table, mask_row,
    )
    vmem = pl.BlockSpec(memory_space=pltpu.VMEM)
    grads = pl.pallas_call(
        finish_kernel,
        name="finish",
        out_shape=[jax.ShapeDtypeStruct(array.shape, F32) for array in owned],
        in_specs=[vmem] * 2,
        out_specs=[vmem] * len(owned),
        compiler_params=pltpu.CompilerParams(vmem_limit_bytes=48 << 20),
    )(gout, gv)
    return (layer_out, grad_in, *grads[:-1], grads[-1][0])


def solution(mesh):
    rows = P(("section", "shard"), None, None)
    first, second, copied = P("shard", None), P(None, "shard"), P()
    return jax.shard_map(
        per_device,
        mesh=mesh,
        in_specs=(rows, rows, copied, copied, copied)
        + (first,) * 4 + (second,) * 2 + (first,) * 7 + (second,) * 3 + (P("shard"),),
        out_specs=(rows, rows)
        + (first,) * 4 + (second,) * 2 + (first,) * 7 + (second,) * 3 + (P("shard"),),
        check_vma=False,
    )
```

profile of v0, /device:TPU:0, one launch (start us, length us, event | category | flops | bytes accessed | tf_op | source)
XLA Modules:
  0.0 301.4 jit_solution(18229132420810875700)
XLA Ops:
  0.7 288.9 %pair.1 = (bf16[2,1024,512]{2,1,0:T(8,128)(2,1)}, f32[2,1024,512]{2,1,0:T(8,128)}, bf16[7,128,2048]{2,1,0:T(8,128)(2,1)}, f32[64,128]{1,0:T(8,128)}, bf16[3,8,2,...) custom-call(bf16[2,1024,512]{2,1,0:T(8,128)(2,1)} %x_in.1, ...), custom_call_target="tpu_custom_call" | custom-call | tf_op jit(solution)/shard_map/pair/pallas_call | solution.py:1052
  289.6 0.0 copy-start
  289.6 2.0 copy-done
  291.6 0.0 copy-start.1
  291.6 0.8 copy-done.1
  292.3 0.0 copy-start.2
  292.4 3.8 %finish.1 = (f32[128,1536]{1,0:T(8,128)}, f32[128,512]{1,0:T(8,128)}, f32[128,2048]{1,0:T(8,128)}, f32[512,512]{1,0:T(8,128)}, f32[2,128]{1,0:T(2,128)}, /*index...) custom-call(bf16[7,128,2048]{2,1,0:T(8,128)(2,1)S(1)} %copy-done, ...), custom_call_target="tpu_custom_call" | custom-call | tf_op jit(solution)/shard_map/finish/pallas_call | solution.py:1175
  296.1 3.0 %copy.43 = bf16[2,1024,512]{2,1,0:T(8,128)(2,1)} copy(bf16[2,1024,512]{2,1,0:T(8,128)(2,1)} %get-tuple-element.80) | data formatting | bytes 4194304
  299.2 0.0 copy-done.2
  299.2 2.0 copy.44
Async XLA Ops:
  289.6 2.0 copy-start
  291.6 0.8 copy-start.1
  292.3 6.8 %copy-start.2 = (f32[2,1024,512]{2,1,0:T(8,128)S(1)}, f32[2,1024,512]{2,1,0:T(8,128)}, u32[]{:S(2)}) copy-start(f32[2,1024,512]{2,1,0:T(8,128)} %get-tuple-element.81) | copy-start | bytes 12582916
where the time goes:
time: 307 us; the launch traced here: 301 us
  Pallas kernels  293 us (95%)
  local copies, waits for them, and re-layouts  7.85 us (3%)
    pallas_call x1, Pallas kernels, run_pair(): pl.pallas_call(kernel, name='pair', out_shape=[out(tokens.shape, BF), out...  289 us
    unnamed x8, local copies, waits for them, and re-layouts  7.85 us

commit v1 on v0

--- a/solution.py
+++ b/solution.py
@@ -25,7 +25,7 @@
 SCALE_LANE = 9
 SMALL_ROWS = 64
 OWNED = 7
-UNITS = 12
+UNITS = 16
 ITEMS = 10
 MESH = pl.DeviceIdType.MESH
 
@@ -234,6 +234,13 @@
 
         lax.fori_loop(0, blocks, step, 0)
 
+    def for_wide_rows(body):
+        def step(r, carry):
+            body(rows_at(r, AB))
+            return carry
+
+        lax.fori_loop(0, length // AB, step, 0)
+
     lane_ids = lax.broadcasted_iota(jnp.int32, (RB, LANES), 1)
 
     def keep_inverse(index, rows, inverse):
@@ -248,13 +255,13 @@
     FREE_Z, FREE_FAR = 2, 3
     trio = 3 * LANES
     half = hidden // 2
-    group = [0, 1, 2, 3, 3, 4, 4, 5, 6, 6, 6, 6]
+    group = [0, 1, 2, 3, 3, 4, 4, 5, 6, 6, 6, 6, 5, 5, 5, 5]
     unit_set = [(0, 1, 0, 1, 0, 1, 0)[g] for g in group]
     first_set = [(0, 1, 2, 0, 1, 2, 0)[g] for g in group]
     halves = [slice(0, half), slice(half, hidden)]
     unit_cols = [slice(0, hidden)] * 3 + halves + halves + [slice(0, hidden)] + [
         slice(3 * width, hidden), slice(0, 2 * trio), slice(2 * trio, 3 * trio), slice(3 * trio, 4 * trio)
-    ]
+    ] * 2
     unit_far_first = [g in (1, 4) for g in group]
     unit_at = [(4, 6, 2, 3, 5, other, own)[g] for g in group]
     opens = [u == 0 or group[u] != group[u - 1] for u in range(UNITS)]
@@ -326,11 +333,6 @@
     def take_far(unit, b):
         if not crosses(unit, b):
             copy_far(unit, b).wait_recv()
-        elif unit == LAST_WHOLE:
-            for part in parts_of_own:
-                cols = unit_cols[part]
-                arrived = r3r.at[1, b, :, cols]
-                reduce_copy(part, AT_FAR + b, arrived, arrived, half_peer).wait_recv()
         elif unit == parts_of_own[0]:
             arrived = r3r.at[0, b]
             reduce_copy(LAST_WHOLE, AT_FAR + b, arrived, arrived, half_peer).wait_recv()
@@ -399,7 +401,7 @@
 
     def sum_far(unit):
         where, cols = unit_set[unit], unit_cols[unit]
-        for b in range(far):
+        for b in range(far - 1 if unit == LAST_WHOLE else far):
             copy_far(unit, b).wait_send()
             take_far(unit, b)
             total = r3s[where, :, cols].astype(F32) + r3r[where, b, :, cols].astype(F32)
@@ -407,6 +409,19 @@
             gain(unit, FREE_FAR + b, lambda following, b=b: [far_list(following)[b]])
             if b + 1 < far:
                 start_far(unit, b + 1)
+        if unit != LAST_WHOLE:
+            copy_keep(unit).start()
+            copy_back(unit).start()
+
+    def sum_cross(unit):
+        part = unit - 4
+        where, cols = unit_set[unit], unit_cols[unit]
+        if unit == 12:
+            copy_far(LAST_WHOLE, far - 1).wait_send()
+        arrived = r3r.at[where, far - 1, :, cols]
+        reduce_copy(part, AT_FAR + far - 1, arrived, arrived, half_peer).wait_recv()
+        total = r3s[where, :, cols].astype(F32) + arrived[...].astype(F32)
+        r3s[where, :, cols] = total.astype(BF)
         copy_keep(unit).start()
         copy_back(unit).start()
 
@@ -491,7 +506,7 @@
             def body(rows, cols=cols):
                 target[rows, cols] = dot(source[rows, :], weight[:, cols]).astype(BF)
 
-            for_rows(body)
+            for_wide_rows(body)
 
     queries = length // AB
 
@@ -719,7 +734,7 @@
         def body(rows):
             dob[rows, :] = dot(dfb[rows, :], wa[which, :, 3 * width :], NT).astype(BF)
 
-        for_rows(body)
+        for_wide_rows(body)
 
     barrier = pltpu.get_barrier_semaphore()
     peers = [(section, later(k)) for k in turns] + [core_peer, side_peer] + far_peers
@@ -905,7 +920,7 @@
             qkv[2, rows, width:], wa[2, :, width : 3 * width], NT
         )
 
-    for_rows(cross_body)
+    for_wide_rows(cross_body)
     sum_core(2)
     norm_back(lambda rows: res[0, rows, :], 0, 2, 1, 3)
     sum_z(0)
@@ -966,6 +981,7 @@
             last_part(11)
             sum_first(10)
             sum_z(8)
+            sum_core(11)
 
         def body(rows):
             value = res[layer, rows, :] + dot(qkv[layer, rows, :], wa[layer, :, : 3 * width], NT)
@@ -977,7 +993,7 @@
             if turn == 0:
                 dp[rows, :] = value.astype(BF)
 
-        for_rows(body)
+        for_wide_rows(body)
         if turn == 0:
             sum_core(7)
             sum_end(3)
@@ -985,15 +1001,22 @@
         else:
             keep_gin = pltpu.make_async_copy(res.at[layer], gin.at[layer], gin_sem.at[0])
             keep_gin.start()
-    sum_core(11)
+    sum_first(11)
     small_start()
     sum_far(8)
     sum_z(9)
+    sum_z(10)
+    sum_far(LAST_WHOLE)
+    sum_cross(12)
     small_core()
     for i in range(QUARTERS):
         send_gin(i).wait()
     load_gin = pltpu.make_async_copy(gin_land, dob, gin_sem.at[1])
     load_gin.start()
+    sum_far(9)
+    sum_cross(13)
+    sum_far(10)
+    sum_cross(14)
     load_gin.wait()
 
     def widen(rows):
@@ -1002,21 +1025,20 @@
     for_rows(widen)
     keep_other = pltpu.make_async_copy(res.at[other], gin.at[other], gin_sem.at[1])
     keep_other.start()
-    sum_first(11)
-    sum_z(10)
-    sum_far(9)
     small_z()
     sum_z(11)
-    sum_far(10)
+    sum_back(8)
+    sum_back(12)
     for b in range(far):
         small_add(b)
     sum_far(11)
-    sum_far(7)
-    for unit in (8, 9, 10, 11):
+    sum_cross(15)
+    for unit in (9, 13, 10, 14):
         sum_back(unit)
     small_add(far)
-    sum_back(7)
-    for unit in (8, 9, 10, 11, 7):
+    sum_back(11)
+    sum_back(15)
+    for unit in (8, 12, 9, 13, 10, 14, 11, 15):
         sum_end(unit)
     keep_other.wait()
     keep_gin.wait()

time: 307 us -> 305 us (level)
  no operation moved by 1% of the time
where the time goes in v1:
time: 305 us; the launch traced here: 299 us
  Pallas kernels  290 us (95%)
  local copies, waits for them, and re-layouts  7.85 us (3%)
    pallas_call x1, Pallas kernels, run_pair(): pl.pallas_call(kernel, name='pair', out_shape=[out(tokens.shape, BF), out...  286 us
    unnamed x8, local copies, waits for them, and re-layouts  7.85 us

profile of v1, /device:TPU:0, one launch (start us, length us, event | category | flops | bytes accessed | tf_op | source)
XLA Modules:
  0.0 298.5 jit_solution(17489797638395674522)
XLA Ops:
  0.7 286.0 %pair.1 = (bf16[2,1024,512]{2,1,0:T(8,128)(2,1)}, f32[2,1024,512]{2,1,0:T(8,128)}, bf16[7,128,2048]{2,1,0:T(8,128)(2,1)}, f32[64,128]{1,0:T(8,128)}, bf16[3,8,2,...) custom-call(bf16[2,1024,512]{2,1,0:T(8,128)(2,1)} %x_in.1, ...), custom_call_target="tpu_custom_call" | custom-call | tf_op jit(solution)/shard_map/pair/pallas_call | solution.py:1074
  286.6 0.0 copy-start
  286.6 2.0 copy-done
  288.7 0.0 copy-start.1
  288.7 0.8 copy-done.1
  289.4 0.0 copy-start.2
  289.4 3.8 %finish.1 = (f32[128,1536]{1,0:T(8,128)}, f32[128,512]{1,0:T(8,128)}, f32[128,2048]{1,0:T(8,128)}, f32[512,512]{1,0:T(8,128)}, f32[2,128]{1,0:T(2,128)}, /*index...) custom-call(bf16[7,128,2048]{2,1,0:T(8,128)(2,1)S(1)} %copy-done, ...), custom_call_target="tpu_custom_call" | custom-call | tf_op jit(solution)/shard_map/finish/pallas_call | solution.py:1197
  293.2 3.0 %copy.43 = bf16[2,1024,512]{2,1,0:T(8,128)(2,1)} copy(bf16[2,1024,512]{2,1,0:T(8,128)(2,1)} %get-tuple-element.80) | data formatting | bytes 4194304
  296.3 0.0 copy-done.2
  296.3 2.0 copy.44
Async XLA Ops:
  286.6 2.0 copy-start
  288.7 0.8 copy-start.1
  289.4 6.8 %copy-start.2 = (f32[2,1024,512]{2,1,0:T(8,128)S(1)}, f32[2,1024,512]{2,1,0:T(8,128)}, u32[]{:S(2)}) copy-start(f32[2,1024,512]{2,1,0:T(8,128)} %get-tuple-element.81) | copy-start | bytes 12582916
